TPU v7x, 128 devices: a whole 4x4x4 slice. The times are simulated.
128 devices in a mesh: prompt: 4 (over z), comp: 32 (over x, y, core).
Axes of the slice: x: 4, y: 4, z: 4, core: 2. Of those that a mesh axis runs over, the one named last changes fastest.
Arguments:
- x_in: bfloat16 [32768, 8192], P(('prompt', 'comp')), may hold values from -6 to 6
- b_in: bfloat16 [32768, 128], P(('prompt', 'comp')), may hold values from -6 to 6
- c_in: bfloat16 [32768, 128], P(('prompt', 'comp')), may hold values from -0.5 to 0.5
- dt_raw: float32 [32768, 128], P(('prompt', 'comp')), may hold values from -6 to 6
- dy_up: bfloat16 [32768, 8192], P(('prompt', 'comp')), may hold values from -6 to 6
- advantages: int32 [32768], P(('prompt', 'comp')), may hold values from -4096 to 4096
- lengths: int32 [128], P(('prompt', 'comp')), may hold values from 64 to 256
- prompt_of: int32 [128, 1], replicated, may hold values from 0 to 3
- a_log: float32 [128], replicated, may hold values from -6.2 to -3
- dt_bias: float32 [128], replicated, may hold values from -1 to 1
- skip_gain: float32 [128], replicated, may hold values from 0.5 to 1.5
- conv_w: float32 [4, 8192], replicated, may hold values from -3 to 3
- conv_b: float32 [8192], replicated, may hold values from -3 to 3
- prompt_state: float32 [4, 128, 64, 128], P('prompt', 'comp'), may hold values from -6 to 6
- prompt_tail: bfloat16 [4, 3, 8192], P('prompt', None, 'comp'), may hold values from -6 to 6
Outputs:
- scores: float32 [32768], P(('prompt', 'comp'))
- grad_x: bfloat16 [32768, 8192], P(('prompt', 'comp'))
- grad_state: float32 [4, 128, 64, 128], P('prompt', 'comp')
- grad_tail: float32 [4, 3, 8192], P('prompt', None, 'comp')
Inputs may be any that keep to these rules, and one draw needn't show every extreme that they name: `prompt_of`: every one of the 4 prompts has at least one slice.
All inputs are finite; a program needn't handle non-finite values.
Results may differ from a plain program's by a relative error of at most 0.002.
Values may be sent and summed in bfloat16 or wider, within the bound.
A program may use at most 256 MiB of HBM per device.

v0:
```python
import jax
import jax.numpy as jnp
from jax import lax
from jax.sharding import PartitionSpec as P


def head_group(
    extended, prefix_state, step_size, decay_rate, skip_part, taps, bias, upstream, affinity, c_rows
):
    tok_rows = step_size.shape[0]
    group_heads = step_size.shape[1]
    head_width = prefix_state.shape[1]
    conv = bias[None, :] + taps[0][None, :] * extended[0:tok_rows]
    for offset in range(1, taps.shape[0]):
        conv = conv + taps[offset][None, :] * extended[offset : offset + tok_rows]
    activated = jax.nn.silu(conv).reshape(tok_rows, group_heads, head_width)
    log_decay = -jnp.cumsum(step_size * decay_rate[None, :], axis=0)
    later_log = log_decay.T[:, :, None]
    earlier_log = log_decay.T[:, None, :]
    causal = jnp.arange(tok_rows)[:, None] >= jnp.arange(tok_rows)[None, :]
    decay_mask = jnp.where(causal[None], jnp.exp(jnp.minimum(later_log - earlier_log, 0.0)), 0.0)
    weighted = decay_mask * affinity[None]
    local_part = jnp.einsum(
        "hts,shp->thp", weighted, activated * step_size[:, :, None], precision=lax.Precision.HIGHEST
    )
    prefix_part = jnp.exp(log_decay)[:, :, None] * jnp.einsum(
        "tn,hpn->thp", c_rows, prefix_state, precision=lax.Precision.HIGHEST
    )
    outputs = local_part + prefix_part + skip_part[None, :, None] * activated
    return jnp.sum(outputs.reshape(tok_rows, -1) * upstream, axis=1)


def local_scores(
    extended,
    prefix_state,
    b_rows,
    c_rows,
    dt_rows,
    upstream,
    token_weight,
    a_log,
    dt_bias,
    skip_gain,
    conv_w,
    conv_b,
):
    tok_rows = dt_rows.shape[0]
    head_count = dt_rows.shape[1]
    head_width = prefix_state.shape[1]
    tail_len = extended.shape[0] - tok_rows
    group_heads = min(16, head_count)
    group_count = head_count // group_heads
    group_width = group_heads * head_width
    c_float = c_rows.astype(jnp.float32)
    affinity = jnp.dot(c_rows, b_rows.T, preferred_element_type=jnp.float32)
    step_size = jax.nn.softplus(dt_rows + dt_bias[None, :])
    decay_rate = jnp.exp(a_log)
    ext_groups = extended.reshape(tok_rows + tail_len, group_count, group_width).transpose(1, 0, 2)
    up_groups = upstream.reshape(tok_rows, group_count, group_width).transpose(1, 0, 2)
    tap_groups = conv_w.reshape(conv_w.shape[0], group_count, group_width).transpose(1, 0, 2)
    bias_groups = conv_b.reshape(group_count, group_width)
    step_groups = step_size.reshape(tok_rows, group_count, group_heads).transpose(1, 0, 2)
    rate_groups = decay_rate.reshape(group_count, group_heads)
    skip_groups = skip_gain.reshape(group_count, group_heads)
    state_groups = prefix_state.reshape(group_count, group_heads, head_width, prefix_state.shape[2])

    def one_group(packed):
        return head_group(
            packed[0],
            packed[1],
            packed[2],
            packed[3],
            packed[4],
            packed[5],
            packed[6],
            packed[7],
            affinity,
            c_float,
        )

    partials = lax.map(
        one_group,
        (
            ext_groups,
            state_groups,
            step_groups,
            rate_groups,
            skip_groups,
            tap_groups,
            bias_groups,
            up_groups,
        ),
    )
    return token_weight * jnp.sum(partials, axis=0)


def body(
    x_in,
    b_in,
    c_in,
    dt_raw,
    dy_up,
    advantages,
    lengths,
    prompt_of,
    a_log,
    dt_bias,
    skip_gain,
    conv_w,
    conv_b,
    prompt_state,
    prompt_tail,
):
    comp_size = lax.axis_size("comp")
    prompt_size = lax.axis_size("prompt")
    head_count = a_log.shape[0]
    head_width = prompt_state.shape[2]
    state_size = prompt_state.shape[3]
    feat_width = x_in.shape[1]
    share_width = prompt_tail.shape[2]
    tok_rows = x_in.shape[0]
    tail_len = prompt_tail.shape[1]
    row_first = lax.axis_index("prompt") * comp_size
    own_index = row_first + lax.axis_index("comp")
    owner_prompt = lax.dynamic_slice(prompt_of, (own_index, 0), (1, 1))[0, 0]
    prompt_ids = jnp.arange(prompt_size, dtype=jnp.int32)
    owner_mask = prompt_ids == owner_prompt
    states_all, tails_all = (
        lax.all_gather(
            prompt_state.astype(jnp.bfloat16), ("prompt", "comp"), axis=1, tiled=True
        ).astype(prompt_state.dtype),
        lax.all_gather(
            prompt_tail.astype(jnp.float32).astype(jnp.bfloat16),
            ("prompt", "comp"),
            axis=2,
            tiled=True,
        ).astype(jnp.float32),
    )
    states_all = states_all.reshape(prompt_size, head_count, head_width, state_size)
    prefix_state = jnp.sum(jnp.where(owner_mask[:, None, None, None], states_all, 0.0), axis=0)
    tails_all = tails_all.reshape(tail_len, prompt_size, feat_width)
    tail = jnp.sum(jnp.where(owner_mask[None, :, None], tails_all, 0.0), axis=1).astype(
        jnp.bfloat16
    )
    positions = jnp.arange(tok_rows, dtype=jnp.int32)
    token_weight = jnp.where(positions < lengths[0], advantages.astype(jnp.float32) / 1024.0, 0.0)
    extended = jnp.concatenate([tail, x_in], axis=0).astype(jnp.float32)

    def scorer(ext_arg, state_arg):
        return local_scores(
            ext_arg,
            state_arg,
            b_in,
            c_in,
            dt_raw,
            dy_up,
            token_weight,
            a_log,
            dt_bias,
            skip_gain,
            conv_w,
            conv_b,
        )

    token_scores, pullback = jax.vjp(scorer, extended, prefix_state)
    grad_ext, grad_prefix = pullback(jnp.ones_like(token_scores))
    grad_x = grad_ext[tail_len:].astype(jnp.bfloat16)
    tail_term = jnp.where(owner_mask[:, None, None], grad_ext[:tail_len][None], 0.0)
    tail_term = tail_term.reshape(prompt_size, tail_len, comp_size, share_width).transpose(
        0, 2, 1, 3
    )
    tail_term = tail_term.reshape(prompt_size * comp_size, tail_len, share_width)
    state_term = jnp.where(owner_mask[:, None, None, None], grad_prefix[None], 0.0)
    state_term = state_term.reshape(prompt_size * head_count, head_width, state_size)
    summed_state, grad_tail = (
        lax.psum_scatter(state_term, ("prompt", "comp"), scatter_dimension=0, tiled=True),
        lax.psum_scatter(tail_term, ("prompt", "comp"), scatter_dimension=0, tiled=True),
    )
    grad_state = summed_state[None]
    return (token_scores, grad_x, grad_state, grad_tail)


def solution(mesh):
    in_specs = (
        P(("prompt", "comp"), None),
        P(("prompt", "comp"), None),
        P(("prompt", "comp"), None),
        P(("prompt", "comp"), None),
        P(("prompt", "comp"), None),
        P(("prompt", "comp")),
        P(("prompt", "comp")),
        P(),
        P(),
        P(),
        P(),
        P(),
        P(),
        P("prompt", "comp", None, None),
        P("prompt", None, "comp"),
    )
    out_specs = (
        P(("prompt", "comp")),
        P(("prompt", "comp"), None),
        P("prompt", "comp", None, None),
        P("prompt", None, "comp"),
    )
    return jax.shard_map(body, mesh=mesh, in_specs=in_specs, out_specs=out_specs, check_vma=False)
```

profile of v0, /device:TPU:1, one launch (start us, length us, event | category | flops | bytes accessed | tf_op | source)
XLA Modules:
  0.0 1321.0 jit_solution(1537081527299632523)
XLA Ops:
  9.0 38.8 %all_gather.6 = bf16[1,3,32768]{2,1,0:T(4,128)(2,1)S(1)} all-gather(bf16[1,3,256]{2,1,0:T(4,128)(2,1)} %param.33), channel_id=1, replica_groups=mesh['prompt'=4,'comp'=32] {'prompt','comp'}, dimensions={2}, use_global_device_ids=true | all-gather | bytes 198144 | tf_op jit(solution)/shard_map/all_gather | solution.py:132
  51.6 6.4 copy.35
  58.0 6.4 copy.39
  68.3 9.7 convert_bitcast_fusion
  78.1 6.7 all-gather.2.cloned.1.call-done
  84.8 8.2 fusion.59
  93.0 282.4 %while.54 = (s32[]{:T(128)}, f32[8,256]{1,0:T(8,128)}, f32[8,1,1024]{2,1,0:T(1,128)S(1)}, f32[8,1,1024]{2,1,0:T(1,128)S(1)}, f32[8,1,1024]{2,1,0:T(1,128)S(1)}, ...) while((s32[]{:T(128)}, f32[8,256]{1,0:T(8,128)}, ...), condition=%wide.region_6.7_spmd.clone.clone, body=%wide.region_2.6_spmd.clone.clone.sunk | while | flops 1225793280 | bytes 35689504 | solution.py:81
  115.2 5.9 fusion.96
  150.4 5.9 fusion.96
  185.6 5.9 fusion.96
  220.9 5.9 fusion.96
  236.6 5.6 constant_dynamic-update-slice_fusion.10
  256.2 5.9 fusion.96
  271.9 5.7 constant_dynamic-update-slice_fusion.10
  291.6 5.9 fusion.96
  307.4 5.7 constant_dynamic-update-slice_fusion.10
  327.1 5.9 fusion.96
  362.3 5.9 fusion.96
  385.3 116.5 %while.53 = (s32[]{:T(128)}, f32[8,259,1024]{1,2,0:T(8,128)}, f32[8,16,64,128]{3,2,1,0:T(8,128)}, f32[8,1,1024]{2,1,0:T(1,128)S(1)}, f32[8,1,16,1]{2,3,1,0:T(1,1...) while((s32[]{:T(128)}, f32[8,259,1024]{1,2,0:T(8,128)}, ...), condition=%wide.region_9.10_spmd, body=%wide.region_8.9_spmd.sunk | while | flops 1212687360 | bytes 27547488 | solution.py:81
  510.5 9.2 bitcast_select_fusion
  519.7 8.1 slice.110
  527.8 6.3 copy.44
  534.1 118.7 %all-reduce.7.cloned.1.call-done = f32[128,3,256]{2,1,0:T(4,128)} async-done(((f32[128,3,256]{2,1,0:T(4,128)}), f32[128,3,256]{2,1,0:T(4,128)}) %all-reduce.7.cloned.1.call-update) | async-done | bytes 393232
  654.1 660.4 %reduce-scatter.2.cloned.1.call-done = f32[4,64,128]{2,1,0:T(8,128)} async-done(((f32[512,64,128]{2,1,0:T(8,128)}), f32[4,64,128]{2,1,0:T(8,128)}) %reduce-scatter.2.cloned.1.call-update) | async-done | bytes 131088 | tf_op jit(solution)/shard_map/reduce_scatter | solution.py:176
  (594 shorter events, 361.4 us)
Async XLA Ops:
  7.2 60.3 %copy-start = (bf16[256,128]{1,0:T(8,128)(2,1)S(1)}, bf16[256,128]{1,0:T(8,128)(2,1)}, u32[]{:S(2)}) copy-start(bf16[256,128]{1,0:T(8,128)(2,1)} %param.20) | copy-start | bytes 196612
  7.2 50.8 %copy-start.4 = (bf16[256,128]{1,0:T(8,128)(2,1)S(1)}, bf16[256,128]{1,0:T(8,128)(2,1)}, u32[]{:S(2)}) copy-start(bf16[256,128]{1,0:T(8,128)(2,1)} %param.21) | copy-start | bytes 196612
  7.2 77.6 %all-gather.2.cloned.1.call-start = ((), (), s32[]{:S(2)}) async-start(), calls=%async_computation.1 | async-start | bytes 8454144 | tf_op jit(solution)/shard_map/all_gather | solution.py:129
  8.8 644.0 %all-reduce.7.cloned.1.call-start = ((), (), s32[]{:S(2)}) async-start(), calls=%async_computation.3 | async-start | bytes 1048576
  50.1 34.8 %copy-start.17 = (pred[4]{0:T(512)(128)(4,1)}, pred[4]{0:T(512)(128)(4,1)S(1)}, u32[]{:S(2)}) copy-start(pred[4]{0:T(512)(128)(4,1)S(1)} %iota_compare_fusion.1) | copy-start | bytes 16
  51.5 13.1 copy-start.8
  51.5 13.1 copy-start.22
  51.6 13.8 %copy-start.20 = (f32[128]{0:T(128)S(1)}, f32[128]{0:T(128)}, u32[]{:S(2)}) copy-start(f32[128]{0:T(128)} %param.29) | copy-start | bytes 1540
  93.0 16.8 %copy-start.2 = (f32[8,256,16]{1,2,0:T(8,128)}, f32[8,256,16]{1,2,0:T(8,128)S(1)}, u32[]{:S(2)}) copy-start(f32[8,256,16]{1,2,0:T(8,128)S(1)} %get-tuple-element.1225) | copy-start | bytes 393220 | tf_op jit(solution)/shard_map/jvp()/while
  128.2 16.8 %copy-start.2 = (f32[8,256,16]{1,2,0:T(8,128)}, f32[8,256,16]{1,2,0:T(8,128)S(1)}, u32[]{:S(2)}) copy-start(f32[8,256,16]{1,2,0:T(8,128)S(1)} %get-tuple-element.1225) | copy-start | bytes 393220 | tf_op jit(solution)/shard_map/jvp()/while
  163.4 16.8 %copy-start.2 = (f32[8,256,16]{1,2,0:T(8,128)}, f32[8,256,16]{1,2,0:T(8,128)S(1)}, u32[]{:S(2)}) copy-start(f32[8,256,16]{1,2,0:T(8,128)S(1)} %get-tuple-element.1225) | copy-start | bytes 393220 | tf_op jit(solution)/shard_map/jvp()/while
  198.6 16.9 %copy-start.2 = (f32[8,256,16]{1,2,0:T(8,128)}, f32[8,256,16]{1,2,0:T(8,128)S(1)}, u32[]{:S(2)}) copy-start(f32[8,256,16]{1,2,0:T(8,128)S(1)} %get-tuple-element.1225) | copy-start | bytes 393220 | tf_op jit(solution)/shard_map/jvp()/while
  233.9 16.9 %copy-start.2 = (f32[8,256,16]{1,2,0:T(8,128)}, f32[8,256,16]{1,2,0:T(8,128)S(1)}, u32[]{:S(2)}) copy-start(f32[8,256,16]{1,2,0:T(8,128)S(1)} %get-tuple-element.1225) | copy-start | bytes 393220 | tf_op jit(solution)/shard_map/jvp()/while
  269.3 17.0 %copy-start.2 = (f32[8,256,16]{1,2,0:T(8,128)}, f32[8,256,16]{1,2,0:T(8,128)S(1)}, u32[]{:S(2)}) copy-start(f32[8,256,16]{1,2,0:T(8,128)S(1)} %get-tuple-element.1225) | copy-start | bytes 393220 | tf_op jit(solution)/shard_map/jvp()/while
  291.6 13.1 copy-start.7
  291.6 13.1 copy-start.10
  291.6 13.1 copy-start.12
  291.6 13.1 copy-start.14
  304.7 17.0 %copy-start.2 = (f32[8,256,16]{1,2,0:T(8,128)}, f32[8,256,16]{1,2,0:T(8,128)S(1)}, u32[]{:S(2)}) copy-start(f32[8,256,16]{1,2,0:T(8,128)S(1)} %get-tuple-element.1225) | copy-start | bytes 393220 | tf_op jit(solution)/shard_map/jvp()/while
  340.1 16.9 %copy-start.2 = (f32[8,256,16]{1,2,0:T(8,128)}, f32[8,256,16]{1,2,0:T(8,128)S(1)}, u32[]{:S(2)}) copy-start(f32[8,256,16]{1,2,0:T(8,128)S(1)} %get-tuple-element.1225) | copy-start | bytes 393220 | tf_op jit(solution)/shard_map/jvp()/while
  362.2 13.1 copy-start.7
  362.3 13.1 copy-start.10
  510.3 804.2 %reduce-scatter.2.cloned.1.call-start = ((), (), s32[]{:S(2)}) async-start(), calls=%async_computation.2 | async-start | bytes 16908288 | tf_op jit(solution)/shard_map/reduce_scatter | solution.py:176
  519.6 794.9 %copy-start.1 = (bf16[256,128]{1,0:T(8,128)(2,1)S(1)}, bf16[256,128]{1,0:T(8,128)(2,1)}, u32[]{:S(2)}) copy-start(bf16[256,128]{1,0:T(8,128)(2,1)} %param.20) | copy-start | bytes 196612
  (86 other events, 650.5 us)
Sparse Core Ops, SparseCore 0:
  11.0 73.7 all-gather.1
  510.5 142.3 all-reduce.6
  655.9 658.5 reduce-scatter.1
where the time goes:
time: 1330 us; the launch traced here: 1320 us
  waiting for transfers between devices  786 us (59%)
  other arithmetic  223 us (17%)
  local copies, waits for them, and re-layouts  137 us (10%)
  matrix products  119 us (9%)
  blocking collectives  38.8 us (3%)
  between operations  14.7 us (1%)
    reduce_scatter x1, waiting for transfers between devices, body(): lax.psum_scatter(state_term, ('prompt', 'comp'), scatter_dimension=0, til...  660 us
    unnamed x4, waiting for transfers between devices  119 us
    dynamic_update_slice x32, other arithmetic, local_scores(): lax.map(one_group, (ext_groups, state_groups, step_groups, rate_groups, s...  116 us
    dot_general x16, matrix products, head_group(): jnp.einsum('hts,shp->thp', weighted, activated * step_size[:, :, None], p...  86.6 us
    all_gather x1, blocking collectives, body(): lax.all_gather(prompt_tail.astype(jnp.float32).astype(jnp.bfloat16), ('pr...  38.8 us
    dynamic_update_slice x32, local copies, waits for them, and re-layouts, local_scores(): lax.map(one_group, (ext_groups, state_groups, step_groups, rate_groups, s...  32.4 us
    dot_general x16, matrix products, head_group(): jnp.einsum('tn,hpn->thp', c_rows, prefix_state, precision=lax.Precision.H...  31.7 us
  transfers between devices with their start and end apart: 3, of which 3 were waited for; matrix products, arithmetic and copies ran while one was open for 4% of the time, Pallas kernels for 0%

commit v1 on v0

v1 whole, which is shorter than its diff:
```python
import functools

import jax
import jax.numpy as jnp
from jax import lax
from jax.experimental import pallas as pl
from jax.experimental.pallas import tpu as pltpu
from jax.sharding import PartitionSpec as P

MESH = pl.DeviceIdType.MESH
F32 = jnp.float32
BF16 = jnp.bfloat16
LN2 = 0.6931471805599453
HIGHEST = lax.Precision.HIGHEST


def split(value):
    high = value.astype(BF16)
    return high, (value - high.astype(F32)).astype(BF16)


def dot(left, right):
    return lax.dot_general(left, right, (((1,), (0,)), ((), ())), preferred_element_type=F32)


def dot_t(left, right):
    return lax.dot_general(left, right, (((1,), (1,)), ((), ())), preferred_element_type=F32)


def gray(digit):
    return digit + digit // 2 - 2 * (digit // 2) * (digit % 2)


def kernel(
    planes,
    comps,
    x_hbm,
    dy_hbm,
    b_ref,
    c_ref,
    dtr_ref,
    adv_ref,
    len_ref,
    prompt_ref,
    alog_ref,
    dtb_ref,
    skip_ref,
    cw_ref,
    cb_ref,
    st_ref,
    tl_ref,
    score_ref,
    gx_hbm,
    gs_ref,
    gt_ref,
    xv,
    dyv,
    gxv,
    zh,
    zl,
    e1,
    e2,
    scale8,
    wcol,
    mth,
    mtl,
    ctv,
    kacc,
    pacc,
    sacc,
    xs,
    gsc,
    sall,
    tall,
    ssend,
    srecv,
    tsend,
    trecv,
    gsend,
    grecv,
    hsend,
    hrecv,
    zsend,
    zrecv,
    loc_sem,
    zs_sem,
    zt_sem,
    zg_sem,
    ss_sem,
    ts_sem,
    gsm_sem,
    hs_sem,
):
    toks = b_ref.shape[0]
    heads = alog_ref.shape[1]
    state = b_ref.shape[1]
    width = xv.shape[1] // comps
    z = lax.axis_index("prompt")
    me = lax.axis_index("comp")
    mx, my, mk = me // 8, (me // 2) % 4, me % 2

    def ahead(j):
        ox, oy, ok = gray(j // 8), gray((j // 2) % 4), j % 2
        return ((mx + ox) % 4 * 4 + (my + oy) % 4) * 2 + (mk + ok) % 2

    def behind(j):
        ox, oy, ok = gray(j // 8), gray((j // 2) % 4), j % 2
        return ((mx + 4 - ox) % 4 * 4 + (my + 4 - oy) % 4) * 2 + (mk + ok) % 2

    def plane_copy(src, dst, sems, j, target):
        return pltpu.make_async_remote_copy(
            src_ref=src,
            dst_ref=dst.at[me],
            send_sem=sems.at[0, j],
            recv_sem=sems.at[1, me],
            device_id=(z, target),
            device_id_type=MESH,
        )

    def plane_arrival(src, dst, sems, source):
        return pltpu.make_async_remote_copy(
            src_ref=src,
            dst_ref=dst.at[source],
            send_sem=sems.at[0, 0],
            recv_sem=sems.at[1, source],
            device_id=(z, source),
            device_id_type=MESH,
        )

    def line_copy(src, dst, sems, step):
        return pltpu.make_async_remote_copy(
            src_ref=src,
            dst_ref=dst.at[z],
            send_sem=sems.at[0, step],
            recv_sem=sems.at[1, z],
            device_id=((z + step) % planes, me),
            device_id_type=MESH,
        )

    def line_arrival(src, dst, sems, step):
        source = (z + planes - step) % planes
        return pltpu.make_async_remote_copy(
            src_ref=src,
            dst_ref=dst.at[source],
            send_sem=sems.at[0, step],
            recv_sem=sems.at[1, source],
            device_id=(source, me),
            device_id_type=MESH,
        )

    load_dy = pltpu.make_async_copy(dy_hbm, dyv, loc_sem.at[0])
    load_x = pltpu.make_async_copy(x_hbm, xv, loc_sem.at[1])
    load_dy.start()
    load_x.start()

    barrier = pltpu.get_barrier_semaphore()

    def greet(j, carry):
        pl.semaphore_signal(barrier, inc=1, device_id=(z, ahead(j)), device_id_type=MESH)
        return carry

    lax.fori_loop(1, comps, greet, 0)
    for step in range(1, planes):
        pl.semaphore_signal(
            barrier, inc=1, device_id=((z + step) % planes, me), device_id_type=MESH
        )

    sall[z] = st_ref[...].astype(BF16)
    xs[0:8, :] = jnp.zeros((8, width), F32)
    xs[5:8, :] = tl_ref[...].astype(F32)
    tall[z] = jnp.concatenate([xs[0:8, :], jnp.zeros((8, width), F32)], axis=0).astype(BF16)

    pl.semaphore_wait(barrier, comps - 1 + planes - 1)
    for step in range(1, planes):
        line_copy(tall.at[z], tall, zt_sem, step).start()
    for step in range(1, planes):
        line_copy(sall.at[z], sall, zs_sem, step).start()

    row = lax.broadcasted_iota(jnp.int32, (toks, toks), 0)
    col = lax.broadcasted_iota(jnp.int32, (toks, toks), 1)
    raw = dtr_ref[...] + dtb_ref[...]
    dt = jnp.maximum(raw, 0.0) + jnp.log1p(jnp.exp(-jnp.abs(raw)))
    total = lax.dot_general(
        jnp.where(row >= col, 1.0, 0.0),
        dt * jnp.exp(alog_ref[...]),
        (((1,), (0,)), ((), ())),
        precision=HIGHEST,
        preferred_element_type=F32,
    )
    power = jnp.floor(total[toks // 2 - 1 : toks // 2, :] * (1.0 / LN2) + 0.5)
    offset = total - power * LN2
    e1[...] = jnp.exp(-offset)
    e2[...] = dt * jnp.exp(offset)
    scale8[...] = jnp.broadcast_to(jnp.exp2(-power), (8, heads))
    weight = jnp.where(
        lax.broadcasted_iota(jnp.int32, (1, toks), 1) < len_ref[0],
        adv_ref[...].astype(F32) / 1024.0,
        0.0,
    )
    wcol[...] = jnp.broadcast_to(
        jnp.sum(jnp.where(row == col, weight, 0.0), axis=1, keepdims=True), (toks, 128)
    )
    high, low = split(jnp.where(row <= col, dot_t(b_ref[...], c_ref[...]), 0.0))
    mth[...] = high
    mtl[...] = low
    ctv[...] = jnp.transpose(c_ref[...].astype(F32)).astype(BF16)
    kacc[...] = jnp.zeros_like(kacc)
    pacc[...] = jnp.zeros_like(pacc)
    sacc[...] = jnp.zeros_like(sacc)
    gsc[0:8, :] = jnp.zeros((8, width), F32)
    gsc[8 + toks :, :] = jnp.zeros((8, width), F32)

    for step in range(1, planes):
        line_arrival(tall.at[z], tall, zt_sem, step).wait_recv()

    def send_tail(j, carry):
        target = ahead(j)
        tsend[j] = tall[prompt_ref[z * comps + target]]
        plane_copy(tsend.at[j], trecv, ts_sem, j, target).start()
        return carry

    lax.fori_loop(1, comps, send_tail, 0)
    trecv[me] = tall[prompt_ref[z * comps + me]]
    for step in range(1, planes):
        line_arrival(sall.at[z], sall, zs_sem, step).wait_recv()

    def send_state(j, carry):
        target = ahead(j)
        ssend[j] = sall[prompt_ref[z * comps + target]]
        plane_copy(ssend.at[j], srecv, ss_sem, j, target).start()
        return carry

    lax.fori_loop(1, comps, send_state, 0)
    srecv[me] = sall[prompt_ref[z * comps + me]]

    half = lax.broadcasted_iota(jnp.int32, (toks, 128), 1) // 64
    half8 = lax.broadcasted_iota(jnp.int32, (8, 128), 1) // 64
    group = width // 64

    def spread(value, index, block):
        parts = [
            jnp.take_along_axis(value, index + (block * group + 2 * i), axis=1)
            for i in range(width // 128)
        ]
        return jnp.concatenate(parts, axis=1)

    def lanes(value):
        return jnp.concatenate([value] * (width // 128), axis=1)

    load_dy.wait()

    def readout(j, carry):
        target = ahead(j)
        cols = pl.ds(pl.multiple_of(target * width, width), width)
        zval = spread(e1[...], half, target) * (lanes(wcol[...]) * dyv[:, cols].astype(F32))
        zhigh, zlow = split(zval)
        zh[target] = zhigh
        zl[target] = zlow
        part = dot(ctv[...], zhigh) + dot(ctv[...], zlow)
        part = part * spread(scale8[...], half8, target)[0:1, :]
        gsend[j] = part.astype(BF16)

        @pl.when(j > 0)
        def _():
            plane_copy(gsend.at[j], grecv, gsm_sem, j, target).start()

        return carry

    lax.fori_loop(0, comps, readout, 0)
    grecv[me] = gsend[0]

    load_x.wait()
    skip8 = jnp.broadcast_to(skip_ref[...], (8, heads))

    def mix(j, carry):
        block = behind(j)
        cols = pl.ds(pl.multiple_of(block * width, width), width)

        @pl.when(j > 0)
        def _():
            plane_arrival(tsend.at[0], trecv, ts_sem, block).wait_recv()

        xs[0:8, :] = trecv[block].astype(F32)[0:8, :]
        xs[8:, :] = xv[:, cols].astype(F32)
        taps = cw_ref[:, cols]
        conv = cb_ref[:, cols] + taps[3:4] * xs[8:, :]
        for k in range(3):
            conv = conv + taps[k : k + 1] * xs[5 + k : 5 + k + toks, :]
        sig = 0.5 * jnp.tanh(0.5 * conv) + 0.5
        act = conv * sig
        slope = sig + act * (1.0 - sig)
        late = spread(e2[...], half, block)
        vhigh, vlow = split(late * act)
        zhigh, zlow = zh[block], zl[block]
        kacc[...] += dot_t(zhigh, vhigh) + dot_t(zlow, vhigh) + dot_t(zhigh, vlow)
        back = dot(mth[...], zhigh) + dot(mth[...], zlow) + dot(mtl[...], zhigh)
        direct = spread(skip8, half8, block)[0:1, :] * (
            lanes(wcol[...]) * dyv[:, cols].astype(F32)
        )
        seen = act * direct
        sacc[...] += seen[:, :128] + seen[:, 128:]
        gsc[8 : 8 + toks, :] = (late * back + direct) * slope
        grad = taps[3:4] * gsc[0 : 8 + toks, :]
        for k in range(3):
            grad = grad + taps[k : k + 1] * gsc[3 - k : 11 - k + toks, :]
        gxv[:, cols] = grad[8:, :].astype(BF16)
        thigh = grad[0:8, :].astype(BF16).astype(F32)
        hsend[j] = jnp.concatenate([thigh, grad[0:8, :] - thigh], axis=0).astype(BF16)

        @pl.when(j > 0)
        def _():
            plane_copy(hsend.at[j], hrecv, hs_sem, j, block).start()

        return carry

    lax.fori_loop(0, comps, mix, 0)
    hrecv[me] = hsend[0]
    store_gx = pltpu.make_async_copy(gxv, gx_hbm, loc_sem.at[2])
    store_gx.start()

    def prefix(j, carry):
        block = behind(j)

        @pl.when(j > 0)
        def _():
            plane_arrival(ssend.at[0], srecv, ss_sem, block).wait_recv()

        scale = spread(scale8[...], half8, block)[0:1, :]
        scale = jnp.broadcast_to(scale, (toks, width)).astype(BF16)
        states = srecv[block]
        pacc[...] += dot(zh[block] * scale, states) + dot(zl[block] * scale, states)
        return carry

    lax.fori_loop(0, comps, prefix, 0)
    aff = dot_t(c_ref[...], b_ref[...])
    scores = (
        jnp.sum(jnp.where(row >= col, aff * kacc[...], 0.0), axis=1, keepdims=True)
        + jnp.sum(sacc[...], axis=1, keepdims=True)
        + jnp.sum(pacc[...] * c_ref[...].astype(F32), axis=1, keepdims=True)
    )
    score_ref[...] = jnp.sum(jnp.where(row == col, scores, 0.0), axis=0, keepdims=True)

    def arrive(j, carry):
        source = behind(j)
        plane_arrival(gsend.at[0], grecv, gsm_sem, source).wait_recv()
        plane_arrival(hsend.at[0], hrecv, hs_sem, source).wait_recv()
        return carry

    lax.fori_loop(1, comps, arrive, 0)

    def gather(r, carry):
        rows = pl.ds(pl.multiple_of(r * 16, 16), 16)
        sums = [jnp.zeros((16, width), F32) for _ in range(planes)]
        for source in range(comps):
            held = prompt_ref[z * comps + source]
            term = grecv[source, rows, :].astype(F32)
            sums = [sums[q] + jnp.where(held == q, term, 0.0) for q in range(planes)]
        for q in range(planes):
            zsend[q, rows, :] = sums[q]
        return carry

    lax.fori_loop(0, state // 16, gather, 0)
    sums = [jnp.zeros((8, width), F32) for _ in range(planes)]
    for source in range(comps):
        held = prompt_ref[z * comps + source]
        term = hrecv[source].astype(F32)
        term = term[0:8, :] + term[8:16, :]
        sums = [sums[q] + jnp.where(held == q, term, 0.0) for q in range(planes)]
    for q in range(planes):
        zsend[q, state:, :] = sums[q]
    for step in range(1, planes):
        line_copy(zsend.at[(z + step) % planes], zrecv, zg_sem, step).start()
    zrecv[z] = zsend[z]

    def leave(j, carry):
        plane_copy(tsend.at[j], trecv, ts_sem, j, ahead(j)).wait_send()
        plane_copy(ssend.at[j], srecv, ss_sem, j, ahead(j)).wait_send()
        plane_copy(gsend.at[j], grecv, gsm_sem, j, ahead(j)).wait_send()
        plane_copy(hsend.at[j], hrecv, hs_sem, j, behind(j)).wait_send()
        return carry

    lax.fori_loop(1, comps, leave, 0)
    for step in range(1, planes):
        line_copy(tall.at[z], tall, zt_sem, step).wait_send()
        line_copy(sall.at[z], sall, zs_sem, step).wait_send()
    for step in range(1, planes):
        line_arrival(zsend.at[0], zrecv, zg_sem, step).wait_recv()
    whole = zrecv[0] + zrecv[1]
    for q in range(2, planes):
        whole = whole + zrecv[q]
    gs_ref[...] = jnp.transpose(whole[0:state, :])
    gt_ref[...] = whole[state + 5 : state + 8, :]
    for step in range(1, planes):
        line_copy(zsend.at[(z + step) % planes], zrecv, zg_sem, step).wait_send()
    store_gx.wait()


def body(planes, comps):
    def run(
        x_in,
        b_in,
        c_in,
        dt_raw,
        dy_up,
        advantages,
        lengths,
        prompt_of,
        a_log,
        dt_bias,
        skip_gain,
        conv_w,
        conv_b,
        prompt_state,
        prompt_tail,
    ):
        toks, feats = x_in.shape
        heads = a_log.shape[0]
        state = b_in.shape[1]
        share = feats // comps
        tail_len = prompt_tail.shape[1]
        vmem = pl.BlockSpec(memory_space=pltpu.VMEM)
        smem = pl.BlockSpec(memory_space=pltpu.SMEM)
        hbm = pl.BlockSpec(memory_space=pl.ANY)
        pair = pltpu.SemaphoreType.DMA((2, comps))
        line = pltpu.SemaphoreType.DMA((2, planes))
        scores, grad_x, grad_state, grad_tail = pl.pallas_call(
            functools.partial(kernel, planes, comps),
            out_shape=(
                jax.ShapeDtypeStruct((1, toks), F32),
                jax.ShapeDtypeStruct((toks, feats), BF16),
                jax.ShapeDtypeStruct((share, state), F32),
                jax.ShapeDtypeStruct((tail_len, share), F32),
            ),
            in_specs=[hbm, hbm, vmem, vmem, vmem, vmem, smem, smem] + [vmem] * 7,
            out_specs=(vmem, hbm, vmem, vmem),
            scratch_shapes=[
                pltpu.VMEM((toks, feats), BF16),
                pltpu.VMEM((toks, feats), BF16),
                pltpu.VMEM((toks, feats), BF16),
                pltpu.VMEM((comps, toks, share), BF16),
                pltpu.VMEM((comps, toks, share), BF16),
                pltpu.VMEM((toks, heads), F32),
                pltpu.VMEM((toks, heads), F32),
                pltpu.VMEM((8, heads), F32),
                pltpu.VMEM((toks, 128), F32),
                pltpu.VMEM((toks, toks), BF16),
                pltpu.VMEM((toks, toks), BF16),
                pltpu.VMEM((state, toks), BF16),
                pltpu.VMEM((toks, toks), F32),
                pltpu.VMEM((toks, state), F32),
                pltpu.VMEM((toks, 128), F32),
                pltpu.VMEM((toks + 8, share), F32),
                pltpu.VMEM((toks + 16, share), F32),
                pltpu.VMEM((planes, share, state), BF16),
                pltpu.VMEM((planes, 16, share), BF16),
                pltpu.VMEM((comps, share, state), BF16),
                pltpu.VMEM((comps, share, state), BF16),
                pltpu.VMEM((comps, 16, share), BF16),
                pltpu.VMEM((comps, 16, share), BF16),
                pltpu.VMEM((comps, state, share), BF16),
                pltpu.VMEM((comps, state, share), BF16),
                pltpu.VMEM((comps, 16, share), BF16),
                pltpu.VMEM((comps, 16, share), BF16),
                pltpu.VMEM((planes, state + 8, share), F32),
                pltpu.VMEM((planes, state + 8, share), F32),
                pltpu.SemaphoreType.DMA((3,)),
                line,
                line,
                line,
                pair,
                pair,
                pair,
                pair,
            ],
            compiler_params=pltpu.CompilerParams(
                collective_id=0, has_side_effects=True, vmem_limit_bytes=56 << 20
            ),
            cost_estimate=pl.CostEstimate(
                flops=10 * toks * toks * feats,
                bytes_accessed=8 * toks * feats,
                transcendentals=toks * feats,
            ),
            name="mixer",
        )(
            x_in,
            dy_up,
            b_in,
            c_in,
            dt_raw,
            advantages.reshape(1, toks),
            lengths,
            prompt_of.reshape(-1),
            a_log.reshape(1, heads),
            dt_bias.reshape(1, heads),
            skip_gain.reshape(1, heads),
            conv_w,
            conv_b.reshape(1, feats),
            prompt_state.reshape(share, state),
            prompt_tail.reshape(tail_len, share),
        )
        return (
            scores.reshape(toks),
            grad_x,
            grad_state.reshape(prompt_state.shape),
            grad_tail.reshape(prompt_tail.shape),
        )

    return run


def solution(mesh):
    planes, comps = mesh.shape["prompt"], mesh.shape["comp"]
    both = P(("prompt", "comp"))
    rows = P(("prompt", "comp"), None)
    state = P("prompt", "comp", None, None)
    tail = P("prompt", None, "comp")
    in_specs = (rows,) * 5 + (both,) * 2 + (P(),) * 6 + (state, tail)
    out_specs = (both, rows, state, tail)
    return jax.shard_map(
        body(planes, comps), mesh=mesh, in_specs=in_specs, out_specs=out_specs, check_vma=False
    )
```

time: 1330 us -> 99.9 us (0.08)
  waiting for transfers between devices: 786 us -> 0 us
  other arithmetic: 223 us -> 0 us
  local copies, waits for them, and re-layouts: 137 us -> 7.82 us
  matrix products: 119 us -> 0 us
  Pallas kernels: 0 us -> 90.6 us
  blocking collectives: 38.8 us -> 0 us
  between operations: 14.7 us -> 1.29 us
    reduce_scatter x1 -> x0, waiting for transfers between devices: 660 us -> none  [body(): lax.psum_scatter(state_term, ('prompt', 'comp'), scatter_dimension=0, til...]
    dot_general x33 -> x0, matrix products: 119 us -> none  [the longest x16 86.6 us: head_group(): jnp.einsum('hts,shp->thp', weighted, activated * step_size[:, :, None], p...]
    unnamed x4 -> x0, waiting for transfers between devices: 119 us -> none
    dynamic_update_slice x32 -> x0, other arithmetic: 116 us -> none  [local_scores(): lax.map(one_group, (ext_groups, state_groups, step_groups, rate_groups, s...]
    pallas_call x0 -> x1, Pallas kernels: none -> 90.6 us  [run(): pl.pallas_call(functools.partial(kernel, planes, comps), out_shape=(jax.S...]
    all_gather x1 -> x0, blocking collectives: 38.8 us -> none  [body(): lax.all_gather(prompt_tail.astype(jnp.float32).astype(jnp.bfloat16), ('pr...]
    mul x25 -> x0, other arithmetic: 37.9 us -> none  [the longest x16 21.1 us: head_group(): conv = conv + taps[offset][None, :] * extended[offset:offset + tok_rows]]
    dynamic_update_slice x32 -> x0, local copies, waits for them, and re-layouts: 32.4 us -> none  [local_scores(): lax.map(one_group, (ext_groups, state_groups, step_groups, rate_groups, s...]
  transfers between devices with their start and end apart: 3 -> 0, of which waited for: 3 -> 0; matrix products, arithmetic and copies ran while one was open for 4% -> 0% of each run, Pallas kernels for 0% -> 0%
where the time goes in v1:
time: 99.9 us; the launch traced here: 99.7 us
  Pallas kernels  90.6 us (91%)
  local copies, waits for them, and re-layouts  7.82 us (8%)
  between operations  1.29 us (1%)
    pallas_call x1, Pallas kernels, run(): pl.pallas_call(functools.partial(kernel, planes, comps), out_shape=(jax.S...  90.6 us
    unnamed x6, local copies, waits for them, and re-layouts  7.82 us

profile of v1, /device:TPU:1, one launch (start us, length us, event | category | flops | bytes accessed | tf_op | source)
XLA Modules:
  0.0 99.7 jit_solution(4818721551051016288)
XLA Ops:
  1.3 90.6 %mixer.1 = (f32[1,256]{1,0:T(1,128)}, bf16[256,8192]{1,0:T(8,128)(2,1)}, f32[256,128]{1,0:T(8,128)}, f32[3,256]{1,0:T(4,128)}) custom-call(bf16[256,8192]{1,0:T(8,128)(2,1)} %x_hbm.1, bf16[256,8192]{1,0:T(8,128)(2,1)} %dy_hbm.1, bf16[256,128]{1,0:T(8,128)(2,1)} %b_ref.1, bf16[256,128]{1,0:T(8,128)(2,1)} %c_ref.1, f32[256,128]{1,0:T(8,128)} %dtr_ref.1, ...), custom_call_target="tpu_custom_call" | custom-call | flops 5368709120 | bytes 16777216 | tf_op jit(solution)/shard_map/mixer/pallas_call | solution.py:426
  91.9 1.3 %copy.19 = f32[1,3,256]{2,0,1:T(1,128)} copy(f32[1,3,256]{2,1,0:T(4,128)} %bitcast.12) | data formatting | bytes 6144
  93.1 1.2 %copy.24 = f32[256]{0:T(256)} copy(f32[256]{0:T(256)} %bitcast.13) | data formatting | bytes 2048
  94.4 0.0 copy-start
  94.4 4.7 %copy.25 = bf16[256,8192]{1,0:T(8,128)(2,1)} copy(bf16[256,8192]{1,0:T(8,128)(2,1)} %get-tuple-element.21) | data formatting | bytes 8388608
  99.0 0.0 copy-done
  99.0 0.7 copy.26
Async XLA Ops:
  94.4 4.7 %copy-start = (f32[256,128]{1,0:T(8,128)S(1)}, f32[256,128]{1,0:T(8,128)}, u32[]{:S(2)}) copy-start(f32[256,128]{1,0:T(8,128)} %get-tuple-element.10) | copy-start | bytes 393220

commit v2 on v1

--- a/solution.py
+++ b/solution.py
@@ -64,12 +64,15 @@
     wcol,
     mth,
     mtl,
-    ctv,
+    lead,
+    first,
     kacc,
     pacc,
     sacc,
     xs,
     gsc,
+    xe,
+    ge,
     sall,
     tall,
     ssend,
@@ -100,11 +103,11 @@
     mx, my, mk = me // 8, (me // 2) % 4, me % 2
 
     def ahead(j):
-        ox, oy, ok = gray(j // 8), gray((j // 2) % 4), j % 2
+        ox, oy, ok = gray(j // 4 % 4), gray((j + j // 4) % 4), j // 16
         return ((mx + ox) % 4 * 4 + (my + oy) % 4) * 2 + (mk + ok) % 2
 
     def behind(j):
-        ox, oy, ok = gray(j // 8), gray((j // 2) % 4), j % 2
+        ox, oy, ok = gray(j // 4 % 4), gray((j + j // 4) % 4), j // 16
         return ((mx + 4 - ox) % 4 * 4 + (my + 4 - oy) % 4) * 2 + (mk + ok) % 2
 
     def plane_copy(src, dst, sems, j, target):
@@ -166,15 +169,9 @@
         )
 
     sall[z] = st_ref[...].astype(BF16)
-    xs[0:8, :] = jnp.zeros((8, width), F32)
-    xs[5:8, :] = tl_ref[...].astype(F32)
-    tall[z] = jnp.concatenate([xs[0:8, :], jnp.zeros((8, width), F32)], axis=0).astype(BF16)
-
-    pl.semaphore_wait(barrier, comps - 1 + planes - 1)
-    for step in range(1, planes):
-        line_copy(tall.at[z], tall, zt_sem, step).start()
-    for step in range(1, planes):
-        line_copy(sall.at[z], sall, zs_sem, step).start()
+    xe[0] = jnp.zeros((16, width), F32)
+    xe[0, 5:8, :] = tl_ref[...].astype(F32)
+    tall[z] = xe[0].astype(BF16)
 
     row = lax.broadcasted_iota(jnp.int32, (toks, toks), 0)
     col = lax.broadcasted_iota(jnp.int32, (toks, toks), 1)
@@ -203,35 +200,20 @@
     high, low = split(jnp.where(row <= col, dot_t(b_ref[...], c_ref[...]), 0.0))
     mth[...] = high
     mtl[...] = low
-    ctv[...] = jnp.transpose(c_ref[...].astype(F32)).astype(BF16)
+    lead[0:state, :] = jnp.transpose(c_ref[...].astype(F32)).astype(BF16)
+    lead[state : state + 16, :] = high[0:16, :]
+    lead[state + 16 :, :] = low[0:16, :]
     kacc[...] = jnp.zeros_like(kacc)
     pacc[...] = jnp.zeros_like(pacc)
     sacc[...] = jnp.zeros_like(sacc)
-    gsc[0:8, :] = jnp.zeros((8, width), F32)
-    gsc[8 + toks :, :] = jnp.zeros((8, width), F32)
-
-    for step in range(1, planes):
-        line_arrival(tall.at[z], tall, zt_sem, step).wait_recv()
-
-    def send_tail(j, carry):
-        target = ahead(j)
-        tsend[j] = tall[prompt_ref[z * comps + target]]
-        plane_copy(tsend.at[j], trecv, ts_sem, j, target).start()
-        return carry
-
-    lax.fori_loop(1, comps, send_tail, 0)
-    trecv[me] = tall[prompt_ref[z * comps + me]]
-    for step in range(1, planes):
-        line_arrival(sall.at[z], sall, zs_sem, step).wait_recv()
-
-    def send_state(j, carry):
-        target = ahead(j)
-        ssend[j] = sall[prompt_ref[z * comps + target]]
-        plane_copy(ssend.at[j], srecv, ss_sem, j, target).start()
-        return carry
-
-    lax.fori_loop(1, comps, send_state, 0)
-    srecv[me] = sall[prompt_ref[z * comps + me]]
+    for u in range(2):
+        gsc[u, toks:, :] = jnp.zeros((8, width), F32)
+
+    pl.semaphore_wait(barrier, comps - 1 + planes - 1)
+    for step in range(1, planes):
+        line_copy(tall.at[z], tall, zt_sem, step).start()
+    for step in range(1, planes):
+        line_copy(sall.at[z], sall, zs_sem, step).start()
 
     half = lax.broadcasted_iota(jnp.int32, (toks, 128), 1) // 64
     half8 = lax.broadcasted_iota(jnp.int32, (8, 128), 1) // 64
@@ -249,96 +231,141 @@
 
     load_dy.wait()
 
-    def readout(j, carry):
+    def readout(i, carry):
+        for u in range(4):
+            j = 4 * i + u
+            target = ahead(j)
+            cols = pl.ds(pl.multiple_of(target * width, width), width)
+            zval = spread(e1[...], half, target) * (lanes(wcol[...]) * dyv[:, cols].astype(F32))
+            zhigh, zlow = split(zval)
+            zh[target] = zhigh
+            zl[target] = zlow
+            part = dot(lead[...], zhigh) + dot(lead[...], zlow)
+            scale = spread(scale8[...], half8, target)[0:1, :]
+            gsend[j] = (part[0:state, :] * scale).astype(BF16)
+            first[target] = part[state : state + 8, :] + part[state + 16 : state + 24, :]
+        for u in range(4):
+            j = 4 * i + u
+
+            def send():
+                plane_copy(gsend.at[j], grecv, gsm_sem, j, ahead(j)).start()
+
+            if u:
+                send()
+            else:
+                pl.when(i > 0)(send)
+        return carry
+
+    lax.fori_loop(0, 2, readout, 0)
+
+    for step in range(1, planes):
+        line_arrival(tall.at[z], tall, zt_sem, step).wait_recv()
+
+    def send_tail(j, carry):
         target = ahead(j)
-        cols = pl.ds(pl.multiple_of(target * width, width), width)
-        zval = spread(e1[...], half, target) * (lanes(wcol[...]) * dyv[:, cols].astype(F32))
-        zhigh, zlow = split(zval)
-        zh[target] = zhigh
-        zl[target] = zlow
-        part = dot(ctv[...], zhigh) + dot(ctv[...], zlow)
-        part = part * spread(scale8[...], half8, target)[0:1, :]
-        gsend[j] = part.astype(BF16)
-
-        @pl.when(j > 0)
-        def _():
-            plane_copy(gsend.at[j], grecv, gsm_sem, j, target).start()
-
-        return carry
-
-    lax.fori_loop(0, comps, readout, 0)
+        tsend[j] = tall[prompt_ref[z * comps + target]]
+        plane_copy(tsend.at[j], trecv, ts_sem, j, target).start()
+        return carry
+
+    lax.fori_loop(1, comps, send_tail, 0)
+    trecv[me] = tall[prompt_ref[z * comps + me]]
+    lax.fori_loop(2, comps // 4, readout, 0)
     grecv[me] = gsend[0]
 
     load_x.wait()
     skip8 = jnp.broadcast_to(skip_ref[...], (8, heads))
 
-    def mix(j, carry):
-        block = behind(j)
-        cols = pl.ds(pl.multiple_of(block * width, width), width)
-
-        @pl.when(j > 0)
-        def _():
-            plane_arrival(tsend.at[0], trecv, ts_sem, block).wait_recv()
-
-        xs[0:8, :] = trecv[block].astype(F32)[0:8, :]
-        xs[8:, :] = xv[:, cols].astype(F32)
-        taps = cw_ref[:, cols]
-        conv = cb_ref[:, cols] + taps[3:4] * xs[8:, :]
-        for k in range(3):
-            conv = conv + taps[k : k + 1] * xs[5 + k : 5 + k + toks, :]
-        sig = 0.5 * jnp.tanh(0.5 * conv) + 0.5
-        act = conv * sig
-        slope = sig + act * (1.0 - sig)
-        late = spread(e2[...], half, block)
-        vhigh, vlow = split(late * act)
-        zhigh, zlow = zh[block], zl[block]
-        kacc[...] += dot_t(zhigh, vhigh) + dot_t(zlow, vhigh) + dot_t(zhigh, vlow)
-        back = dot(mth[...], zhigh) + dot(mth[...], zlow) + dot(mtl[...], zhigh)
-        direct = spread(skip8, half8, block)[0:1, :] * (
-            lanes(wcol[...]) * dyv[:, cols].astype(F32)
-        )
-        seen = act * direct
-        sacc[...] += seen[:, :128] + seen[:, 128:]
-        gsc[8 : 8 + toks, :] = (late * back + direct) * slope
-        grad = taps[3:4] * gsc[0 : 8 + toks, :]
-        for k in range(3):
-            grad = grad + taps[k : k + 1] * gsc[3 - k : 11 - k + toks, :]
-        gxv[:, cols] = grad[8:, :].astype(BF16)
-        thigh = grad[0:8, :].astype(BF16).astype(F32)
-        hsend[j] = jnp.concatenate([thigh, grad[0:8, :] - thigh], axis=0).astype(BF16)
-
-        @pl.when(j > 0)
-        def _():
-            plane_copy(hsend.at[j], hrecv, hs_sem, j, block).start()
-
-        return carry
-
-    lax.fori_loop(0, comps, mix, 0)
+    def arrive_tail(j, carry):
+        plane_arrival(tsend.at[0], trecv, ts_sem, behind(j)).wait_recv()
+        return carry
+
+    lax.fori_loop(1, comps, arrive_tail, 0)
+
+    def gate(conv):
+        rise = jnp.tanh(conv) + 1.0
+        act = conv * rise
+        return act, rise + act * (2.0 - rise)
+
+    def edge(i, carry):
+        for u in range(4):
+            j = 4 * i + u
+            block = ahead(j)
+            cols = pl.ds(pl.multiple_of(block * width, width), width)
+            xe[u, 0:8, :] = trecv[block].astype(F32)[0:8, :]
+            xe[u, 8:16, :] = xv[0:16, cols].astype(F32)[0:8, :]
+            taps = 0.5 * cw_ref[:, cols]
+            conv = 0.5 * cb_ref[:, cols] + taps[3:4] * xe[u, 8:16, :]
+            for k in range(3):
+                conv = conv + taps[k : k + 1] * xe[u, 5 + k : 13 + k, :]
+            slope = gate(conv)[1]
+            direct = spread(skip8, half8, block) * (
+                lanes(wcol[0:8, :]) * dyv[0:16, cols].astype(F32)[0:8, :]
+            )
+            ge[u, 0:8, :] = jnp.zeros((8, width), F32)
+            ge[u, 8:16, :] = (spread(e2[0:8, :], half8, block) * first[block] + direct) * slope
+            grad = taps[3:4] * ge[u, 0:8, :]
+            for k in range(3):
+                grad = grad + taps[k : k + 1] * ge[u, 3 - k : 11 - k, :]
+            high = grad.astype(BF16).astype(F32)
+            hsend[j] = jnp.concatenate([high, grad - high], axis=0).astype(BF16)
+        for u in range(4):
+            j = 4 * i + u
+
+            def send():
+                plane_copy(hsend.at[j], hrecv, hs_sem, j, ahead(j)).start()
+
+            if u:
+                send()
+            else:
+                pl.when(i > 0)(send)
+        return carry
+
+    lax.fori_loop(0, comps // 4, edge, 0)
     hrecv[me] = hsend[0]
+
+    for step in range(1, planes):
+        line_arrival(sall.at[z], sall, zs_sem, step).wait_recv()
+
+    def send_state(j, carry):
+        target = ahead(j)
+        ssend[j] = sall[prompt_ref[z * comps + target]]
+        plane_copy(ssend.at[j], srecv, ss_sem, j, target).start()
+        return carry
+
+    lax.fori_loop(1, comps, send_state, 0)
+    srecv[me] = sall[prompt_ref[z * comps + me]]
+
+    def mix(i, carry):
+        for u in range(2):
+            block = 2 * i + u
+            cols = pl.ds(pl.multiple_of(block * width, width), width)
+            xs[u, 0:8, :] = trecv[block].astype(F32)[0:8, :]
+            xs[u, 8:, :] = xv[:, cols].astype(F32)
+            taps = 0.5 * cw_ref[:, cols]
+            conv = 0.5 * cb_ref[:, cols] + taps[3:4] * xs[u, 8:, :]
+            for k in range(3):
+                conv = conv + taps[k : k + 1] * xs[u, 5 + k : 5 + k + toks, :]
+            act, slope = gate(conv)
+            late = spread(e2[...], half, block)
+            vhigh, vlow = split(late * act)
+            zhigh, zlow = zh[block], zl[block]
+            kacc[...] += dot_t(zhigh, vhigh) + dot_t(zlow, vhigh) + dot_t(zhigh, vlow)
+            back = dot(mth[...], zhigh) + dot(mth[...], zlow) + dot(mtl[...], zhigh)
+            direct = spread(skip8, half8, block)[0:1, :] * (
+                lanes(wcol[...]) * dyv[:, cols].astype(F32)
+            )
+            seen = act * direct
+            sacc[...] += seen[:, :128] + seen[:, 128:]
+            gsc[u, 0:toks, :] = (late * back + direct) * slope
+            grad = taps[3:4] * gsc[u, 0:toks, :]
+            for k in range(3):
+                grad = grad + taps[k : k + 1] * gsc[u, 3 - k : 3 - k + toks, :]
+            gxv[:, cols] = grad.astype(BF16)
+        return carry
+
+    lax.fori_loop(0, comps // 2, mix, 0)
     store_gx = pltpu.make_async_copy(gxv, gx_hbm, loc_sem.at[2])
     store_gx.start()
-
-    def prefix(j, carry):
-        block = behind(j)
-
-        @pl.when(j > 0)
-        def _():
-            plane_arrival(ssend.at[0], srecv, ss_sem, block).wait_recv()
-
-        scale = spread(scale8[...], half8, block)[0:1, :]
-        scale = jnp.broadcast_to(scale, (toks, width)).astype(BF16)
-        states = srecv[block]
-        pacc[...] += dot(zh[block] * scale, states) + dot(zl[block] * scale, states)
-        return carry
-
-    lax.fori_loop(0, comps, prefix, 0)
-    aff = dot_t(c_ref[...], b_ref[...])
-    scores = (
-        jnp.sum(jnp.where(row >= col, aff * kacc[...], 0.0), axis=1, keepdims=True)
-        + jnp.sum(sacc[...], axis=1, keepdims=True)
-        + jnp.sum(pacc[...] * c_ref[...].astype(F32), axis=1, keepdims=True)
-    )
-    score_ref[...] = jnp.sum(jnp.where(row == col, scores, 0.0), axis=0, keepdims=True)
 
     def arrive(j, carry):
         source = behind(j)
@@ -372,11 +399,51 @@
         line_copy(zsend.at[(z + step) % planes], zrecv, zg_sem, step).start()
     zrecv[z] = zsend[z]
 
+    def prefix(i, carry):
+        for u in range(4):
+            j = 4 * i + u
+
+            def arrive_state():
+                plane_arrival(ssend.at[0], srecv, ss_sem, behind(j)).wait_recv()
+
+            if u:
+                arrive_state()
+            else:
+                pl.when(i > 0)(arrive_state)
+        total = pacc[...]
+        for u in range(4):
+            block = behind(4 * i + u)
+            scales = [
+                jnp.take_along_axis(
+                    scale8[...], jnp.full((8, 128), block * group + g, jnp.int32), axis=1
+                )[0:1, :]
+                for g in range(group)
+            ]
+            states = jnp.concatenate(
+                [
+                    srecv[block, 64 * g : 64 * g + 64, :].astype(F32) * scales[g]
+                    for g in range(group)
+                ],
+                axis=0,
+            ).astype(BF16)
+            total = total + dot(zh[block], states) + dot(zl[block], states)
+        pacc[...] = total
+        return carry
+
+    lax.fori_loop(0, comps // 4, prefix, 0)
+    aff = dot_t(c_ref[...], b_ref[...])
+    scores = (
+        jnp.sum(jnp.where(row >= col, aff * kacc[...], 0.0), axis=1, keepdims=True)
+        + jnp.sum(sacc[...], axis=1, keepdims=True)
+        + jnp.sum(pacc[...] * c_ref[...].astype(F32), axis=1, keepdims=True)
+    )
+    score_ref[...] = jnp.sum(jnp.where(row == col, scores, 0.0), axis=0, keepdims=True)
+
     def leave(j, carry):
         plane_copy(tsend.at[j], trecv, ts_sem, j, ahead(j)).wait_send()
         plane_copy(ssend.at[j], srecv, ss_sem, j, ahead(j)).wait_send()
         plane_copy(gsend.at[j], grecv, gsm_sem, j, ahead(j)).wait_send()
-        plane_copy(hsend.at[j], hrecv, hs_sem, j, behind(j)).wait_send()
+        plane_copy(hsend.at[j], hrecv, hs_sem, j, ahead(j)).wait_send()
         return carry
 
     lax.fori_loop(1, comps, leave, 0)
@@ -389,10 +456,19 @@
     for q in range(2, planes):
         whole = whole + zrecv[q]
     gs_ref[...] = jnp.transpose(whole[0:state, :])
-    gt_ref[...] = whole[state + 5 : state + 8, :]
+    gt_ref[...] = whole[state:, :]
     for step in range(1, planes):
         line_copy(zsend.at[(z + step) % planes], zrecv, zg_sem, step).wait_send()
     store_gx.wait()
+
+
+def finish(gx_in, score_in, gs_in, gt_in, score_ref, gx_ref, gs_ref, gt_ref, sem):
+    copy = pltpu.make_async_copy(gx_in, gx_ref, sem)
+    copy.start()
+    score_ref[...] = score_in[...]
+    gs_ref[...] = gs_in[...]
+    gt_ref[...] = gt_in[5:8, :].reshape(gt_ref.shape)
+    copy.wait()
 
 
 def body(planes, comps):
@@ -420,6 +496,7 @@
         tail_len = prompt_tail.shape[1]
         vmem = pl.BlockSpec(memory_space=pltpu.VMEM)
         smem = pl.BlockSpec(memory_space=pltpu.SMEM)
+        off = pl.BlockSpec(memory_space=pltpu.HBM)
         hbm = pl.BlockSpec(memory_space=pl.ANY)
         pair = pltpu.SemaphoreType.DMA((2, comps))
         line = pltpu.SemaphoreType.DMA((2, planes))
@@ -429,9 +506,9 @@
                 jax.ShapeDtypeStruct((1, toks), F32),
                 jax.ShapeDtypeStruct((toks, feats), BF16),
                 jax.ShapeDtypeStruct((share, state), F32),
-                jax.ShapeDtypeStruct((tail_len, share), F32),
+                jax.ShapeDtypeStruct((8, share), F32),
             ),
-            in_specs=[hbm, hbm, vmem, vmem, vmem, vmem, smem, smem] + [vmem] * 7,
+            in_specs=[off, off, vmem, vmem, vmem, vmem, smem, smem] + [vmem] * 7,
             out_specs=(vmem, hbm, vmem, vmem),
             scratch_shapes=[
                 pltpu.VMEM((toks, feats), BF16),
@@ -445,12 +522,15 @@
                 pltpu.VMEM((toks, 128), F32),
                 pltpu.VMEM((toks, toks), BF16),
                 pltpu.VMEM((toks, toks), BF16),
-                pltpu.VMEM((state, toks), BF16),
+                pltpu.VMEM((state + 32, toks), BF16),
+                pltpu.VMEM((comps, 8, share), F32),
                 pltpu.VMEM((toks, toks), F32),
                 pltpu.VMEM((toks, state), F32),
                 pltpu.VMEM((toks, 128), F32),
-                pltpu.VMEM((toks + 8, share), F32),
-                pltpu.VMEM((toks + 16, share), F32),
+                pltpu.VMEM((2, toks + 8, share), F32),
+                pltpu.VMEM((2, toks + 8, share), F32),
+                pltpu.VMEM((4, 16, share), F32),
+                pltpu.VMEM((4, 16, share), F32),
                 pltpu.VMEM((planes, share, state), BF16),
                 pltpu.VMEM((planes, 16, share), BF16),
                 pltpu.VMEM((comps, share, state), BF16),
@@ -498,11 +578,25 @@
             prompt_state.reshape(share, state),
             prompt_tail.reshape(tail_len, share),
         )
+        scores, grad_x, grad_state, grad_tail = pl.pallas_call(
+            finish,
+            out_shape=(
+                jax.ShapeDtypeStruct((1, toks), F32),
+                jax.ShapeDtypeStruct((toks, feats), BF16),
+                jax.ShapeDtypeStruct((share, state), F32),
+                jax.ShapeDtypeStruct((tail_len, 1, share), F32),
+            ),
+            in_specs=[off, vmem, vmem, vmem],
+            out_specs=(vmem, off, vmem, vmem),
+            scratch_shapes=[pltpu.SemaphoreType.DMA],
+            compiler_params=pltpu.CompilerParams(vmem_limit_bytes=4 << 20),
+            name="finish",
+        )(grad_x, scores, grad_state, grad_tail)
         return (
             scores.reshape(toks),
             grad_x,
             grad_state.reshape(prompt_state.shape),
-            grad_tail.reshape(prompt_tail.shape),
+            grad_tail.reshape(tail_len, 1, share).transpose(1, 0, 2),
         )
 
     return run

time: 99.9 us -> 82.2 us (0.82)
  the two profiles are of different devices: /device:TPU:1 before, /device:TPU:97 now
where the time goes in v2:
time: 82.2 us; the launch traced here: 82 us
  Pallas kernels  76.2 us (93%)
  local copies, waits for them, and re-layouts  4.44 us (5%)
  between operations  1.3 us (2%)
    pallas_call x1, Pallas kernels, run(): pl.pallas_call(functools.partial(kernel, planes, comps), out_shape=(jax.S...  73.6 us
    unnamed x8, local copies, waits for them, and re-layouts  4.44 us
    pallas_call x1, Pallas kernels, run(): pl.pallas_call(finish, out_shape=(jax.ShapeDtypeStruct((1, toks), F32), j...  2.68 us

profile of v2, /device:TPU:97, one launch (start us, length us, event | category | flops | bytes accessed | tf_op | source)
XLA Modules:
  0.0 82.0 jit_solution(12968486569508935782)
XLA Ops:
  1.3 73.6 %mixer.1 = (f32[1,256]{1,0:T(1,128)}, bf16[256,8192]{1,0:T(8,128)(2,1)}, f32[256,128]{1,0:T(8,128)}, f32[8,256]{1,0:T(8,128)}) custom-call(bf16[256,8192]{1,0:T(8,128)(2,1)} %x_hbm.1, bf16[256,8192]{1,0:T(8,128)(2,1)} %dy_hbm.1, bf16[256,128]{1,0:T(8,128)(2,1)} %b_ref.1, bf16[256,128]{1,0:T(8,128)(2,1)} %c_ref.1, f32[256,128]{1,0:T(8,128)} %dtr_ref.1, ...), custom_call_target="tpu_custom_call" | custom-call | flops 5368709120 | bytes 16777216 | tf_op jit(solution)/shard_map/mixer/pallas_call | solution.py:503
  74.8 0.0 copy-start
  74.9 2.2 %copy-done = bf16[256,8192]{1,0:T(8,128)(2,1)S(1)} copy-done((bf16[256,8192]{1,0:T(8,128)(2,1)S(1)}, bf16[256,8192]{1,0:T(8,128)(2,1)}, u32[]{:S(2)}) %copy-start) | copy-done | bytes 4194328
  77.0 0.0 copy-start.1
  77.0 0.9 %copy-done.1 = f32[256,128]{1,0:T(8,128)S(1)} copy-done((f32[256,128]{1,0:T(8,128)S(1)}, f32[256,128]{1,0:T(8,128)}, u32[]{:S(2)}) %copy-start.1) | copy-done | bytes 131096
  77.9 0.0 copy-start.2
  77.9 0.7 copy-done.2
  78.6 0.0 copy-start.3
  78.6 0.7 copy-done.3
  79.3 2.7 %finish.1 = (f32[1,256]{1,0:T(1,128)}, bf16[256,8192]{1,0:T(8,128)(2,1)}, f32[256,128]{1,0:T(8,128)}, f32[3,1,256]{2,1,0:T(1,128)}) custom-call(bf16[256,8192]{1,0:T(8,128)(2,1)S(1)} %copy-done, f32[1,256]{1,0:T(1,128)S(1)} %copy-done.3, f32[256,128]{1,0:T(8,128)S(1)} %copy-done.1, f32[8,256]{1,0:T(8,128)S(1)} %copy-done.2), custom_call_target="tpu_custom_call" | custom-call | tf_op jit(solution)/shard_map/finish/pallas_call | solution.py:581
Async XLA Ops:
  74.8 2.2 %copy-start = (bf16[256,8192]{1,0:T(8,128)(2,1)S(1)}, bf16[256,8192]{1,0:T(8,128)(2,1)}, u32[]{:S(2)}) copy-start(bf16[256,8192]{1,0:T(8,128)(2,1)} %get-tuple-element.12.gx_in) | copy-start | bytes 12582916
  77.0 0.9 %copy-start.1 = (f32[256,128]{1,0:T(8,128)S(1)}, f32[256,128]{1,0:T(8,128)}, u32[]{:S(2)}) copy-start(f32[256,128]{1,0:T(8,128)} %get-tuple-element.14.gs_in) | copy-start | bytes 393220
  77.9 0.7 copy-start.2
  78.6 0.7 copy-start.3

commit v3 on v2

--- a/solution.py
+++ b/solution.py
@@ -27,8 +27,9 @@
     return lax.dot_general(left, right, (((1,), (1,)), ((), ())), preferred_element_type=F32)
 
 
-def gray(digit):
-    return digit + digit // 2 - 2 * (digit // 2) * (digit % 2)
+def offsets(j):
+    row = lax.rem(lax.div(j, 4), 4)
+    return lax.rem(j, 4), lax.rem(j + row, 4), lax.div(j, 16)
 
 
 def kernel(
@@ -100,15 +101,15 @@
     width = xv.shape[1] // comps
     z = lax.axis_index("prompt")
     me = lax.axis_index("comp")
-    mx, my, mk = me // 8, (me // 2) % 4, me % 2
+    mx, my, mk = lax.div(me, 8), lax.rem(lax.div(me, 2), 4), lax.rem(me, 2)
 
     def ahead(j):
-        ox, oy, ok = gray(j // 4 % 4), gray((j + j // 4) % 4), j // 16
-        return ((mx + ox) % 4 * 4 + (my + oy) % 4) * 2 + (mk + ok) % 2
+        ox, oy, ok = offsets(jnp.int32(j))
+        return (lax.rem(mx + ox, 4) * 4 + lax.rem(my + oy, 4)) * 2 + lax.rem(mk + ok, 2)
 
     def behind(j):
-        ox, oy, ok = gray(j // 4 % 4), gray((j + j // 4) % 4), j // 16
-        return ((mx + 4 - ox) % 4 * 4 + (my + 4 - oy) % 4) * 2 + (mk + ok) % 2
+        ox, oy, ok = offsets(jnp.int32(j))
+        return (lax.rem(mx + 4 - ox, 4) * 4 + lax.rem(my + 4 - oy, 4)) * 2 + lax.rem(mk + ok, 2)
 
     def plane_copy(src, dst, sems, j, target):
         return pltpu.make_async_remote_copy(
@@ -276,7 +277,7 @@
     skip8 = jnp.broadcast_to(skip_ref[...], (8, heads))
 
     def arrive_tail(j, carry):
-        plane_arrival(tsend.at[0], trecv, ts_sem, behind(j)).wait_recv()
+        plane_arrival(tsend.at[0], trecv, ts_sem, lax.rem(me + j, comps)).wait_recv()
         return carry
 
     lax.fori_loop(1, comps, arrive_tail, 0)
@@ -368,7 +369,7 @@
     store_gx.start()
 
     def arrive(j, carry):
-        source = behind(j)
+        source = lax.rem(me + j, comps)
         plane_arrival(gsend.at[0], grecv, gsm_sem, source).wait_recv()
         plane_arrival(hsend.at[0], hrecv, hs_sem, source).wait_recv()
         return carry
@@ -398,6 +399,16 @@
     for step in range(1, planes):
         line_copy(zsend.at[(z + step) % planes], zrecv, zg_sem, step).start()
     zrecv[z] = zsend[z]
+
+    beside = lax.rem(me + 1, comps)
+
+    def leave(j, carry):
+        plane_copy(tsend.at[j], trecv, ts_sem, j, beside).wait_send()
+        plane_copy(gsend.at[j], grecv, gsm_sem, j, beside).wait_send()
+        plane_copy(hsend.at[j], hrecv, hs_sem, j, beside).wait_send()
+        return carry
+
+    lax.fori_loop(1, comps, leave, 0)
 
     def prefix(i, carry):
         for u in range(4):
@@ -439,14 +450,11 @@
     )
     score_ref[...] = jnp.sum(jnp.where(row == col, scores, 0.0), axis=0, keepdims=True)
 
-    def leave(j, carry):
-        plane_copy(tsend.at[j], trecv, ts_sem, j, ahead(j)).wait_send()
-        plane_copy(ssend.at[j], srecv, ss_sem, j, ahead(j)).wait_send()
-        plane_copy(gsend.at[j], grecv, gsm_sem, j, ahead(j)).wait_send()
-        plane_copy(hsend.at[j], hrecv, hs_sem, j, ahead(j)).wait_send()
-        return carry
-
-    lax.fori_loop(1, comps, leave, 0)
+    def leave_state(j, carry):
+        plane_copy(ssend.at[j], srecv, ss_sem, j, beside).wait_send()
+        return carry
+
+    lax.fori_loop(1, comps, leave_state, 0)
     for step in range(1, planes):
         line_copy(tall.at[z], tall, zt_sem, step).wait_send()
         line_copy(sall.at[z], sall, zs_sem, step).wait_send()
@@ -456,19 +464,33 @@
     for q in range(2, planes):
         whole = whole + zrecv[q]
     gs_ref[...] = jnp.transpose(whole[0:state, :])
-    gt_ref[...] = whole[state:, :]
+    gt_ref[...] = whole[state + 5 : state + 8, :].reshape(gt_ref.shape)
     for step in range(1, planes):
         line_copy(zsend.at[(z + step) % planes], zrecv, zg_sem, step).wait_send()
     store_gx.wait()
 
 
-def finish(gx_in, score_in, gs_in, gt_in, score_ref, gx_ref, gs_ref, gt_ref, sem):
-    copy = pltpu.make_async_copy(gx_in, gx_ref, sem)
-    copy.start()
-    score_ref[...] = score_in[...]
-    gs_ref[...] = gs_in[...]
-    gt_ref[...] = gt_in[5:8, :].reshape(gt_ref.shape)
-    copy.wait()
+def finish(parts, *refs):
+    sources, targets, held, sems = refs[0:4], refs[4:8], refs[8:12], refs[12]
+    rows = held[1].shape[0] // parts
+    spans = [(1, pl.ds(rows * i, rows)) for i in range(parts)] + [
+        (i, pl.ds(0, held[i].shape[0])) for i in (0, 2, 3)
+    ]
+    loads = [
+        pltpu.make_async_copy(sources[i].at[span], held[i].at[span], sems.at[0, n])
+        for n, (i, span) in enumerate(spans)
+    ]
+    stores = [
+        pltpu.make_async_copy(held[i].at[span], targets[i].at[span], sems.at[1, n])
+        for n, (i, span) in enumerate(spans)
+    ]
+    for load in loads:
+        load.start()
+    for load, store in zip(loads, stores):
+        load.wait()
+        store.start()
+    for store in stores:
+        store.wait()
 
 
 def body(planes, comps):
@@ -506,7 +528,7 @@
                 jax.ShapeDtypeStruct((1, toks), F32),
                 jax.ShapeDtypeStruct((toks, feats), BF16),
                 jax.ShapeDtypeStruct((share, state), F32),
-                jax.ShapeDtypeStruct((8, share), F32),
+                jax.ShapeDtypeStruct((tail_len, 1, share), F32),
             ),
             in_specs=[off, off, vmem, vmem, vmem, vmem, smem, smem] + [vmem] * 7,
             out_specs=(vmem, hbm, vmem, vmem),
@@ -579,19 +601,25 @@
             prompt_tail.reshape(tail_len, share),
         )
         scores, grad_x, grad_state, grad_tail = pl.pallas_call(
-            finish,
+            functools.partial(finish, 8),
             out_shape=(
                 jax.ShapeDtypeStruct((1, toks), F32),
                 jax.ShapeDtypeStruct((toks, feats), BF16),
                 jax.ShapeDtypeStruct((share, state), F32),
                 jax.ShapeDtypeStruct((tail_len, 1, share), F32),
             ),
-            in_specs=[off, vmem, vmem, vmem],
-            out_specs=(vmem, off, vmem, vmem),
-            scratch_shapes=[pltpu.SemaphoreType.DMA],
-            compiler_params=pltpu.CompilerParams(vmem_limit_bytes=4 << 20),
+            in_specs=[off] * 4,
+            out_specs=(off,) * 4,
+            scratch_shapes=[
+                pltpu.VMEM((1, toks), F32),
+                pltpu.VMEM((toks, feats), BF16),
+                pltpu.VMEM((share, state), F32),
+                pltpu.VMEM((tail_len, 1, share), F32),
+                pltpu.SemaphoreType.DMA((2, 11)),
+            ],
+            compiler_params=pltpu.CompilerParams(vmem_limit_bytes=56 << 20),
             name="finish",
-        )(grad_x, scores, grad_state, grad_tail)
+        )(scores, grad_x, grad_state, grad_tail)
         return (
             scores.reshape(toks),
             grad_x,

time: 82.2 us -> 73.7 us (0.90)
  the two profiles are of different devices: /device:TPU:97 before, /device:TPU:1 now
where the time goes in v3:
time: 73.7 us; the launch traced here: 73.5 us
  Pallas kernels  72.2 us (98%)
  between operations  1.29 us (2%)
    pallas_call x1, Pallas kernels, run(): pl.pallas_call(functools.partial(kernel, planes, comps), out_shape=(jax.S...  68.6 us
    pallas_call x1, Pallas kernels, run(): pl.pallas_call(functools.partial(finish, 8), out_shape=(jax.ShapeDtypeStr...  3.67 us

profile of v3, /device:TPU:1, one launch (start us, length us, event | category | flops | bytes accessed | tf_op | source)
XLA Modules:
  0.0 73.5 jit_solution(17416514171312494215)
XLA Ops:
  1.3 68.6 %mixer.1 = (f32[1,256]{1,0:T(1,128)}, bf16[256,8192]{1,0:T(8,128)(2,1)}, f32[256,128]{1,0:T(8,128)}, f32[3,1,256]{2,1,0:T(1,128)}) custom-call(bf16[256,8192]{1,0:T(8,128)(2,1)} %x_hbm.1, bf16[256,8192]{1,0:T(8,128)(2,1)} %dy_hbm.1, bf16[256,128]{1,0:T(8,128)(2,1)} %b_ref.1, bf16[256,128]{1,0:T(8,128)(2,1)} %c_ref.1, f32[256,128]{1,0:T(8,128)} %dtr_ref.1, ...), custom_call_target="tpu_custom_call" | custom-call | flops 5368709120 | bytes 16777216 | tf_op jit(solution)/shard_map/mixer/pallas_call | solution.py:525
  69.9 3.7 %finish.1 = (f32[1,256]{1,0:T(1,128)}, bf16[256,8192]{1,0:T(8,128)(2,1)}, f32[256,128]{1,0:T(8,128)}, f32[3,1,256]{2,1,0:T(1,128)}) custom-call(f32[1,256]{1,0:T(1,128)} %get-tuple-element.12.refs_0_, bf16[256,8192]{1,0:T(8,128)(2,1)} %get-tuple-element.13.refs_1_, f32[256,128]{1,0:T(8,128)} %get-tuple-element.14.refs_2_, f32[3,1,256]{2,1,0:T(1,128)} %get-tuple-element.15.refs_3_), custom_call_target="tpu_custom_call" | custom-call | tf_op jit(solution)/shard_map/finish/pallas_call | solution.py:603

commit v4 on v3

--- a/solution.py
+++ b/solution.py
@@ -191,7 +191,7 @@
     e2[...] = dt * jnp.exp(offset)
     scale8[...] = jnp.broadcast_to(jnp.exp2(-power), (8, heads))
     weight = jnp.where(
-        lax.broadcasted_iota(jnp.int32, (1, toks), 1) < len_ref[0],
+        lax.broadcasted_iota(jnp.int32, (1, toks), 1) < len_ref[...],
         adv_ref[...].astype(F32) / 1024.0,
         0.0,
     )
@@ -530,7 +530,7 @@
                 jax.ShapeDtypeStruct((share, state), F32),
                 jax.ShapeDtypeStruct((tail_len, 1, share), F32),
             ),
-            in_specs=[off, off, vmem, vmem, vmem, vmem, smem, smem] + [vmem] * 7,
+            in_specs=[off, off, vmem, vmem, vmem, vmem, vmem, smem] + [vmem] * 7,
             out_specs=(vmem, hbm, vmem, vmem),
             scratch_shapes=[
                 pltpu.VMEM((toks, feats), BF16),
@@ -590,7 +590,7 @@
             c_in,
             dt_raw,
             advantages.reshape(1, toks),
-            lengths,
+            lengths.reshape(1, 1),
             prompt_of.reshape(-1),
             a_log.reshape(1, heads),
             dt_bias.reshape(1, heads),

time: 73.7 us -> 73.7 us (level)
  no operation moved by 1% of the time
where the time goes in v4:
time: 73.7 us; the launch traced here: 73.5 us
  Pallas kernels  72.2 us (98%)
  between operations  1.29 us (2%)
    pallas_call x1, Pallas kernels, run(): pl.pallas_call(functools.partial(kernel, planes, comps), out_shape=(jax.S...  68.6 us
    pallas_call x1, Pallas kernels, run(): pl.pallas_call(functools.partial(finish, 8), out_shape=(jax.ShapeDtypeStr...  3.67 us

profile of v4, /device:TPU:1, one launch (start us, length us, event | category | flops | bytes accessed | tf_op | source)
XLA Modules:
  0.0 73.5 jit_solution(2238132832531369199)
XLA Ops:
  1.3 68.6 %mixer.1 = (f32[1,256]{1,0:T(1,128)}, bf16[256,8192]{1,0:T(8,128)(2,1)}, f32[256,128]{1,0:T(8,128)}, f32[3,1,256]{2,1,0:T(1,128)}) custom-call(bf16[256,8192]{1,0:T(8,128)(2,1)} %x_hbm.1, bf16[256,8192]{1,0:T(8,128)(2,1)} %dy_hbm.1, bf16[256,128]{1,0:T(8,128)(2,1)} %b_ref.1, bf16[256,128]{1,0:T(8,128)(2,1)} %c_ref.1, f32[256,128]{1,0:T(8,128)} %dtr_ref.1, ...), custom_call_target="tpu_custom_call" | custom-call | flops 5368709120 | bytes 16777216 | tf_op jit(solution)/shard_map/mixer/pallas_call | solution.py:525
  69.9 3.7 %finish.1 = (f32[1,256]{1,0:T(1,128)}, bf16[256,8192]{1,0:T(8,128)(2,1)}, f32[256,128]{1,0:T(8,128)}, f32[3,1,256]{2,1,0:T(1,128)}) custom-call(f32[1,256]{1,0:T(1,128)} %get-tuple-element.12.refs_0_, bf16[256,8192]{1,0:T(8,128)(2,1)} %get-tuple-element.13.refs_1_, f32[256,128]{1,0:T(8,128)} %get-tuple-element.14.refs_2_, f32[3,1,256]{2,1,0:T(1,128)} %get-tuple-element.15.refs_3_), custom_call_target="tpu_custom_call" | custom-call | tf_op jit(solution)/shard_map/finish/pallas_call | solution.py:603
